TPU v7x, 256 devices: a whole 4x4x8 slice. The times are simulated.
256 devices in a mesh: fit: 8 (over x, core), pair: 32 (over z, y).
Axes of the slice: x: 4, y: 4, z: 8, core: 2. Of those that a mesh axis runs over, the one named last changes fastest.
Arguments:
- b_ints: bfloat16 [32, 61440, 256], P(None, ('fit', 'pair')), may hold values from -0.375 to 0.375
- dom_blocks: int32 [32, 4], replicated, may hold values from 0 to 624, as said below
- pair_list: int32 [384, 2], P('pair'), may hold values from 0 to 31, as said below
- fock_tab: bfloat16 [625, 4096], replicated, may hold values from -0.875 to 0.875
- vir_energy: float32 [40000], replicated, may hold values from 1 to 3
- occ_energy: float32 [32], replicated, may hold values from -2 to -0.3
- t_amp: bfloat16 [384, 256, 256], P('pair'), may hold values from -3 to 3
Outputs:
- residual: float32 [384, 256, 256], P('pair', 'fit')
- t_new: bfloat16 [384, 256, 256], P('pair', 'fit')
Inputs may be any that keep to these rules, and one draw needn't show every extreme that they name: `dom_blocks`: each row names 4 different blocks; some row names block 0 and block 624. `pair_list`: the 12 pairs of owner g (rows g * 12 to (g + 1) * 12 - 1) have both orbitals among (4 g + r) mod 32 for r = 0 to 3; each owner's first pair is (4 g mod 32, (4 g + 3) mod 32).
All inputs are finite; a program needn't handle non-finite values.
Results may differ from a plain program's by a relative error of at most 0.0015.
Values may be sent and summed in bfloat16 or wider, within the bound.
No kernel may reach another device: no remote copies, remote signals or barrier semaphores. Data moves between devices by JAX's collectives and lax.ppermute only.
A program may use at most 384 MiB of HBM per device.

v0:
```python
import jax
import jax.numpy as jnp
from jax import lax
from jax.sharding import PartitionSpec as P


def domain_fock(orbit, dom_blocks, fock_tab, vir_energy):
    blocks = dom_blocks[orbit]
    block_count = blocks.shape[0]
    fock_tiles = jnp.take(fock_tab, blocks, axis=0).reshape(block_count, 64, 64).astype(jnp.float32)
    diag_unit = jnp.eye(block_count, dtype=jnp.float32)
    fock_full = (fock_tiles[:, :, None, :] * diag_unit[:, None, :, None]).reshape(
        block_count * 64, block_count * 64
    )
    virt_ids = (blocks[:, None] * 64 + jnp.arange(64, dtype=jnp.int32)[None, :]).reshape(-1)
    energy = jnp.take(vir_energy, virt_ids)
    fock_full = fock_full + jnp.diag(energy)
    return (fock_full, jnp.diagonal(fock_full))


def local(b_ints, dom_blocks, pair_list, fock_tab, vir_energy, occ_energy, t_amp):
    fit_count = lax.axis_size("fit")
    dom_width = t_amp.shape[2]
    rows_fit = dom_width // fit_count
    local_fit = b_ints.shape[1]
    orbit_total = b_ints.shape[0]
    orb_a = pair_list[:, 0]
    orb_b = pair_list[:, 1]
    pair_count = lax.axis_size("pair")
    group_base = jnp.arange(pair_count, dtype=jnp.int32) * 4
    group_ids = (group_base[:, None] + jnp.arange(4, dtype=jnp.int32)[None, :]) % orbit_total
    outgoing = jnp.take(b_ints, group_ids.reshape(-1), axis=0)
    outgoing = outgoing.reshape(1, pair_count, 4, local_fit, dom_width)
    own_base = lax.axis_index("pair") * 4
    slot_a = (orb_a - own_base) % orbit_total
    slot_b = (orb_b - own_base) % orbit_total

    def group_products(group):
        members = group[0]

        def one_pair(slots):
            left = lax.dynamic_index_in_dim(members, slots[0], 0, keepdims=False)
            right = lax.dynamic_index_in_dim(members, slots[1], 0, keepdims=False)
            return jnp.einsum("qa,qb->ab", left, right, preferred_element_type=jnp.float32)

        return lax.map(one_pair, (slot_a, slot_b))

    k_partial = jax.vmap(group_products)(
        lax.all_to_all(outgoing, "pair", split_axis=1, concat_axis=3, tiled=True)
    )
    k_rows = lax.psum_scatter(k_partial[0], "fit", scatter_dimension=1, tiled=True)
    row_start = lax.axis_index("fit") * rows_fit
    fock_a, diag_a = jax.vmap(lambda orbit: domain_fock(orbit, dom_blocks, fock_tab, vir_energy))(
        orb_a
    )
    fock_b, diag_b = jax.vmap(lambda orbit: domain_fock(orbit, dom_blocks, fock_tab, vir_energy))(
        orb_b
    )
    fock_rows = lax.dynamic_slice_in_dim(fock_a, row_start, rows_fit, 1)
    diag_rows = lax.dynamic_slice_in_dim(diag_a, row_start, rows_fit, 1)
    amplitude = t_amp.astype(jnp.float32)
    amp_rows = lax.dynamic_slice_in_dim(amplitude, row_start, rows_fit, 1)
    pair_shift = jnp.take(occ_energy, orb_a) + jnp.take(occ_energy, orb_b)
    left_term = jnp.einsum("nac,ncb->nab", fock_rows, amplitude, precision=lax.Precision.HIGHEST)
    right_term = jnp.einsum("nac,ncb->nab", amp_rows, fock_b, precision=lax.Precision.HIGHEST)
    residual = k_rows + left_term + right_term - pair_shift[:, None, None] * amp_rows
    denominator = diag_rows[:, :, None] + diag_b[:, None, :] - pair_shift[:, None, None]
    t_new = (amp_rows - residual / denominator).astype(jnp.bfloat16)
    return (residual, t_new)


def solution(mesh):
    placed = (
        P(None, ("fit", "pair"), None),
        P(),
        P("pair", None),
        P(),
        P(),
        P(),
        P("pair", None, None),
    )
    return jax.shard_map(
        local,
        mesh=mesh,
        in_specs=placed,
        out_specs=(P("pair", "fit", None), P("pair", "fit", None)),
        check_vma=False,
    )
```

profile of v0, /device:TPU:26, one launch (start us, length us, event | category | flops | bytes accessed | tf_op | source)
XLA Modules:
  0.0 679.7 jit_solution(12264417744221989114)
XLA Ops:
  7.5 9.6 %gather_fusion = bf16[128,240,256]{2,1,0:T(8,128)(2,1)} fusion(bf16[32,240,256]{2,1,0:T(8,128)(2,1)} %param.15, s32[1024]{0:T(1024)S(1)} %pad_clamp_fusion.4), kind=kCustom, calls=%fused_computation.6 | custom fusion | bytes 31457792 | tf_op jit(solution)/shard_map/jit(_take)/gather | solution.py:32
  17.1 13.6 %broadcast_select_fusion = bf16[1,32,4,240,256]{4,3,2,0,1:T(8,128)(2,1)} fusion(bf16[1,32,4,240,256]{4,3,2,0,1:T(8,128)(2,1)} %bitcast.89, pred[32,4]{1,0:T(8,128)(4,1)S(1)} %compare_and_fusion), kind=kLoop, calls=%fused_computation.21 | loop fusion | flops 7864320 | bytes 31457408 | tf_op jit(solution)/shard_map/jit(_take)/select_n | solution.py:32
  30.7 11.7 %all-to-all-start = ((bf16[1,32,4,240,256]{4,3,2,0,1:T(8,128)(2,1)}), bf16[1,32,4,240,256]{4,3,2,0,1:T(8,128)(2,1)}, u32[]{:S(2)}, u32[]{:S(2)}) async-start(bf16[1,32,4,240,256]{4,3,2,0,1:T(8,128)(2,1)} %broadcast_select_fusion), calls=%async_computation | async-start | bytes 31457280 | tf_op jit(solution)/shard_map/all_to_all | solution.py:49
  42.5 372.8 %all-to-all-done = bf16[1,32,4,240,256]{4,3,2,0,1:T(8,128)(2,1)} async-done(((bf16[1,32,4,240,256]{4,3,2,0,1:T(8,128)(2,1)}), bf16[1,32,4,240,256]{4,3,2,0,1:T(8,128)(2,1)}, u32[]{:S(2)}, u32[]{:S(2)}) %all-to-all-start) | async-done | bytes 15728672 | tf_op jit(solution)/shard_map/all_to_all | solution.py:49
  415.3 13.2 %copy.31 = bf16[1,32,4,240,256]{4,3,1,2,0:T(8,128)(2,1)} copy(bf16[1,32,4,240,256]{4,3,2,0,1:T(8,128)(2,1)} %all-to-all-done) | data formatting | bytes 31457280 | tf_op jit(solution)/shard_map/all_to_all | solution.py:49
  428.5 120.2 %while.12 = (s32[]{:T(128)}, f32[12,1,256,256]{3,2,1,0:T(8,128)}, s32[12]{0:T(128)S(1)}, bf16[1,4,7680,256]{3,2,1,0:T(8,128)(2,1)}, s32[12]{0:T(128)S(1)}, /*index=5*/s32[]{:T(128)}, s32[]{:T(128)}, s32[]{:T(128)}) while((s32[]{:T(128)}, f32[12,1,256,256]{3,2,1,0:T(8,128)}, s32[12]{0:T(128)S(1)}, bf16[1,4,7680,256]{3,2,1,0:T(8,128)(2,1)}, ...), condition=%wide.region_1.2_spmd, body=%wide.region_0.1_spmd.sunk | while | flops 1006632960 | bytes 8126693 | solution.py:46
  428.5 0.6 dynamic_slice.33
  431.1 0.6 dynamic_slice.34
  433.3 5.3 fusion.44
  438.5 0.6 dynamic_slice.33
  441.1 0.6 dynamic_slice.34
  443.3 5.3 fusion.44
  448.6 0.6 dynamic_slice.33
  451.1 0.6 dynamic_slice.34
  453.3 5.3 fusion.44
  458.5 0.6 dynamic_slice.33
  461.1 0.6 dynamic_slice.34
  463.3 5.3 fusion.44
  468.6 0.6 dynamic_slice.33
  471.1 0.6 dynamic_slice.34
  473.3 5.3 fusion.44
  478.6 0.6 dynamic_slice.33
  481.1 0.6 dynamic_slice.34
  483.3 5.3 fusion.44
  488.6 0.6 dynamic_slice.33
  491.1 0.6 dynamic_slice.34
  493.3 5.3 fusion.44
  498.6 0.6 dynamic_slice.33
  501.2 0.6 dynamic_slice.34
  503.4 5.3 fusion.44
  508.7 0.6 dynamic_slice.33
  511.2 0.6 dynamic_slice.34
  513.4 5.2 fusion.44
  518.7 0.6 dynamic_slice.33
  521.2 0.6 dynamic_slice.34
  523.4 5.3 fusion.44
  528.7 0.6 dynamic_slice.33
  533.4 5.3 fusion.44
  538.7 0.6 dynamic_slice.33
  543.4 5.3 fusion.44
  548.7 0.7 copy-done.3
  549.5 0.6 gather_fusion.1
  550.2 4.3 gather_fusion.5
  554.9 0.8 reshape.228
  555.6 3.8 mul.85
  559.5 6.9 %mul.86 = f32[12,256,256]{2,1,0:T(8,128)} reshape(f32[12,4,64,4,64]{4,3,2,1,0:T(4,128)} %mul.85) | data formatting | bytes 6291456 | tf_op jit(solution)/shard_map/vmap()/mul | solution.py:12
  566.6 0.6 gather_fusion.2
  567.5 17.4 %gather_fusion.8 = f32[3072]{0:T(1024)S(1)} fusion(f32[40000]{0:T(1024)S(1)} %copy-done, s32[3072]{0:T(1024)S(1)} %broadcast_clamp_fusion), kind=kCustom, calls=%fused_computation.4.clone | custom fusion | bytes 36864 | tf_op jit(solution)/shard_map/vmap(jit(_take))/gather | solution.py:16
  584.9 17.4 %gather_fusion.6 = f32[3072]{0:T(1024)S(1)} fusion(f32[40000]{0:T(1024)S(1)} %copy-done, s32[3072]{0:T(1024)S(1)} %broadcast_clamp_fusion.1), kind=kCustom, calls=%fused_computation.1.clone | custom fusion | bytes 36864 | tf_op jit(solution)/shard_map/vmap(jit(_take))/gather | solution.py:16
  602.5 1.0 mul.88
  603.6 4.3 gather_fusion.7
  608.3 0.8 reshape.229
  609.1 3.8 mul.93
  612.9 6.9 %mul.94 = f32[12,256,256]{2,1,0:T(8,128)} reshape(f32[12,4,64,4,64]{4,3,2,1,0:T(4,128)} %mul.93) | data formatting | bytes 6291456 | tf_op jit(solution)/shard_map/vmap()/mul | solution.py:12
  619.9 4.6 select_add_fusion.1
  624.4 16.5 %copy.36 = f32[12,256,256]{0,2,1:T(8,128)} copy(f32[12,256,256]{2,1,0:T(8,128)S(1)} %get-tuple-element.68) | data formatting | bytes 6291456 | tf_op jit(solution)/shard_map/vmap()/add | solution.py:17
  641.0 2.3 gather_fusion.4
  643.4 17.9 %copy.34 = f32[12,256,256]{0,2,1:T(8,128)} copy(f32[12,256,256]{2,1,0:T(8,128)} %get-tuple-element.67) | data formatting | bytes 6291456 | tf_op jit(solution)/shard_map/vmap()/add | solution.py:17
  661.3 3.0 gather_fusion.3
  664.3 0.7 dynamic-slice_bitcast_fusion
  665.1 0.7 gather_fusion.9
  665.8 0.7 gather_fusion.10
  666.4 2.9 fusion.20
  669.3 3.5 fusion.18
  (68 shorter events, 3.4 us)
Async XLA Ops:
  7.2 560.3 %copy-start = (f32[40000]{0:T(1024)S(1)}, f32[40000]{0:T(1024)}, u32[]{:S(2)}) copy-start(f32[40000]{0:T(1024)} %param.19) | copy-start | bytes 480004
  30.7 11.7 %copy-start.2 = (s32[12,2]{0,1:T(2,128)S(1)}, s32[12,2]{0,1:T(2,128)}, u32[]{:S(2)}) copy-start(s32[12,2]{0,1:T(2,128)} %param.17) | copy-start | bytes 292
  30.7 384.6 %all-to-all-start = ((bf16[1,32,4,240,256]{4,3,2,0,1:T(8,128)(2,1)}), bf16[1,32,4,240,256]{4,3,2,0,1:T(8,128)(2,1)}, u32[]{:S(2)}, u32[]{:S(2)}) async-start(bf16[1,32,4,240,256]{4,3,2,0,1:T(8,128)(2,1)} %broadcast_select_fusion), calls=%async_computation | async-start | bytes 31457280 | tf_op jit(solution)/shard_map/all_to_all | solution.py:49
  42.4 626.9 %reduce-scatter.2.cloned.1.call-start = ((), (), s32[]{:S(2)}) async-start(), calls=%async_computation.2 | async-start | bytes 3538944 | tf_op jit(solution)/shard_map/reduce_scatter | solution.py:51
  548.7 0.7 copy-start.3
  643.4 21.7 %copy-start.1 = (f32[32]{0:T(128)S(1)}, f32[32]{0:T(128)}, u32[]{:S(2)}) copy-start(f32[32]{0:T(128)} %param.20) | copy-start | bytes 388
Sparse Core Ops, SparseCore 0:
  548.8 36.6 reduce-scatter.1
where the time goes:
time: 681 us; the launch traced here: 680 us
  waiting for transfers between devices  373 us (55%)
  local copies, waits for them, and re-layouts  149 us (22%)
  matrix products  69.6 us (10%)
  loops' own time  43.2 us (6%)
  other arithmetic  19 us (3%)
  between operations  14.3 us (2%)
  starting transfers between devices  11.7 us (2%)
    all_to_all x1, waiting for transfers between devices, local(): lax.all_to_all(outgoing, 'pair', split_axis=1, concat_axis=3, tiled=True)  373 us
    dot_general x12, matrix products, one_pair(): jnp.einsum('qa,qb->ab', left, right, preferred_element_type=jnp.float32)  63.3 us
    another operation x1, loops' own time, group_products(): return lax.map(one_pair, (slot_a, slot_b))  43.2 us
    gather x4, local copies, waits for them, and re-layouts, domain_fock(): energy = jnp.take(vir_energy, virt_ids)  34.8 us
    add x2, local copies, waits for them, and re-layouts, domain_fock(): fock_full = fock_full + jnp.diag(energy)  34.5 us
    mul x6, local copies, waits for them, and re-layouts, domain_fock(): fock_tiles[:, :, None, :] * diag_unit[:, None, :, None]  22.7 us
    dynamic_slice x24, local copies, waits for them, and re-layouts, group_products(): return lax.map(one_pair, (slot_a, slot_b))  13.7 us
    select_n x2, other arithmetic, local(): outgoing = jnp.take(b_ints, group_ids.reshape(-1), axis=0)  13.6 us
  transfers between devices with their start and end apart: 2, of which 1 were waited for; matrix products, arithmetic and copies ran while one was open for 18% of the time, Pallas kernels for 0%

commit v1 on v0

v1 whole, which is shorter than its diff:
```python
import functools

import jax
import jax.numpy as jnp
from jax import lax
from jax.experimental import pallas as pl
from jax.experimental.pallas import tpu as pltpu
from jax.sharding import Mesh, PartitionSpec as P

FIT = ("x", "core")
PAIR = ("zq", "zp", "y")
OWN = ("zp", "y")
SCALE = 4.0
ORBITALS = 4
HALF = jnp.float16


HALVES = (
    ((0, 0), (0, 1), (1, 0), (1, 1), (0, 2), (2, 0), (0, 3), (3, 0)),
    ((1, 2), (2, 1), (1, 3), (3, 1), (2, 2), (2, 3), (3, 2), (3, 3)),
)


def up(zq):
    return zq ^ 1


def down(zq):
    return ((zq + 1) ^ 1) - 1


def swapped(value, partner):
    return lax.ppermute(value, "zq", [(i, partner(i) % 4) for i in range(4)])


def gram_kernel(blocks, place, ints, *refs):
    keeps, send, full = refs[:4], refs[4], refs[5]
    x, core = place[0], place[1]

    def rows_of(orbital):
        return ints[:, orbital].reshape(-1, ints.shape[-1])

    def emit(at):
        for dx in range(4):
            start = pl.multiple_of(64 * lax.rem(x + dx, 4), 64)
            keeps[dx][at] = full[pl.ds(start + 32 * core, 32), :]
            send[dx, at] = full[pl.ds(start + 32 * (1 - core), 32), :]

    for i in range(ORBITALS):
        wanted = [j for j in range(i, ORBITALS) if (i, j) in blocks]
        if not wanted:
            continue
        left = rows_of(i).T
        for j in wanted:
            product = jnp.dot(left, rows_of(j), preferred_element_type=jnp.float32) * SCALE
            full[...] = product
            emit(blocks.index((i, j)))
            if i != j:
                full[...] = product.T
                emit(blocks.index((j, i)))


def gram(place, ints, blocks):
    nb, width = len(blocks), ints.shape[-1]
    piece = (nb, 32, width)
    whole = pl.BlockSpec(memory_space=pltpu.VMEM)
    *keep, send = pl.pallas_call(
        functools.partial(gram_kernel, blocks),
        out_shape=[jax.ShapeDtypeStruct(piece, jnp.float32)] * 4
        + [jax.ShapeDtypeStruct((4, *piece), jnp.float32)],
        in_specs=[pl.BlockSpec(memory_space=pltpu.SMEM), whole],
        out_specs=[whole] * 5,
        scratch_shapes=[pltpu.VMEM((width, width), jnp.float32)],
        compiler_params=pltpu.CompilerParams(vmem_limit_bytes=40 << 20),
        cost_estimate=pl.CostEstimate(
            flops=2 * nb * width * width * ints.shape[0] * ints.shape[2],
            bytes_accessed=nb * width * width * 8,
            transcendentals=0,
        ),
    )(place, ints)
    return keep, send


def fock_kernel(slots, place, occ, fock, energy, amp, w_ref, den_ref, row_ref):
    p = pl.program_id(0)
    block = place[3]
    off = pl.multiple_of(32 * place[1], 32)
    sa, sb = slots[2 * p], slots[2 * p + 1]
    shift = occ[sa] + occ[sb]
    rows = amp[0, pl.ds(off, 32), :]
    rows32 = rows.astype(jnp.float32)
    fa = fock[4 * sa + block, pl.ds(off, 32), :]
    ea = energy[4 * sa + block]
    left = jnp.dot(fa, amp[0], preferred_element_type=jnp.float32)
    on_diag = lax.broadcasted_iota(jnp.int32, (32, 64), 1) == (
        lax.broadcasted_iota(jnp.int32, (32, 64), 0) + off
    )
    ea_col = jnp.sum(jnp.where(on_diag, ea, 0.0), axis=1, keepdims=True)
    fa_col = jnp.sum(jnp.where(on_diag, fa.astype(jnp.float32), 0.0), axis=1, keepdims=True)
    unit = lax.broadcasted_iota(jnp.int32, (64, 64), 0) == lax.broadcasted_iota(
        jnp.int32, (64, 64), 1
    )
    right, eb, db = [], [], []
    for k in range(4):
        fb = fock[4 * sb + k]
        right.append(
            jnp.dot(rows[:, 64 * k : 64 * k + 64], fb, preferred_element_type=jnp.float32)
        )
        eb.append(energy[4 * sb + k])
        fb_diag = jnp.sum(jnp.where(unit, fb.astype(jnp.float32), 0.0), axis=0, keepdims=True)
        db.append(fb_diag + eb[-1])
    right = jnp.concatenate(right, axis=1) + rows32 * jnp.concatenate(eb, axis=1)
    left = left + ea_col * rows32
    w_ref[0] = left + right - shift * rows32
    den_ref[0] = (fa_col + ea_col) + jnp.concatenate(db, axis=1) - shift
    row_ref[0] = rows32


def fock_terms(slots, place, occ, fock, energy, t_amp):
    pairs = t_amp.shape[0]
    out = jax.ShapeDtypeStruct((pairs, 32, 256), jnp.float32)
    row_spec = pl.BlockSpec((1, 32, 256), lambda p, *_: (p, 0, 0))
    return pl.pallas_call(
        fock_kernel,
        out_shape=(out, out, out),
        grid_spec=pltpu.PrefetchScalarGridSpec(
            num_scalar_prefetch=3,
            grid=(pairs,),
            in_specs=[
                pl.BlockSpec((16, 64, 64), lambda p, *_: (0, 0, 0)),
                pl.BlockSpec((16, 1, 64), lambda p, *_: (0, 0, 0)),
                pl.BlockSpec((1, 64, 256), lambda p, slots, place, occ: (p, place[3], 0)),
            ],
            out_specs=(row_spec, row_spec, row_spec),
        ),
        cost_estimate=pl.CostEstimate(
            flops=pairs * 32 * 64 * 256 * 4, bytes_accessed=pairs * 32 * 256 * 16, transcendentals=0
        ),
    )(slots, place, occ, fock, energy, t_amp)


def final_kernel(pairs, index, a_ref, b_ref, w_ref, den_ref, row_ref, res_ref, new_ref, full):
    size = a_ref.shape[0]
    full[:size] = a_ref[...]
    full[size:] = b_ref[...]
    for p in range(pairs):
        res = full[index[p]] * (1.0 / SCALE) + w_ref[p]
        res_ref[p] = res
        new_ref[p] = (row_ref[p] - res / den_ref[p]).astype(jnp.bfloat16)


def finish(index, sums, w, den, rows):
    pairs = w.shape[0]
    whole = pl.BlockSpec(memory_space=pltpu.VMEM)
    smem = pl.BlockSpec(memory_space=pltpu.SMEM)
    return pl.pallas_call(
        functools.partial(final_kernel, pairs),
        out_shape=(
            jax.ShapeDtypeStruct(w.shape, jnp.float32),
            jax.ShapeDtypeStruct(w.shape, jnp.bfloat16),
        ),
        in_specs=[smem] + [whole] * 5,
        out_specs=(whole, whole),
        scratch_shapes=[pltpu.VMEM((ORBITALS * ORBITALS, *w.shape[1:]), jnp.float32)],
    )(index, *sums, w, den, rows)


def shifted(value, axis, by):
    count = lax.axis_size(axis)
    return lax.ppermute(value, axis, [(i, (i + by) % count) for i in range(count)])


def to_float(value):
    return value.astype(jnp.float32)


def over_cores(keep, send):
    other = shifted(send.astype(HALF), "core", 1)
    both = [keep[d] + to_float(other[d]) for d in range(4)]
    return both[0], [both[d].astype(HALF) for d in (2, 1, 3)]


def over_x(pieces):
    return [shifted(piece, "x", d) for piece, d in zip(pieces, (2, 1, 3))]


def local(b_ints, dom_blocks, pair_list, fock_tab, vir_energy, occ_energy, t_amp):
    barrier = lax.optimization_barrier
    x, core, group = lax.axis_index("x"), lax.axis_index("core"), lax.axis_index(OWN)
    place = jnp.stack([x, core, x, x]).astype(jnp.int32)
    first = ORBITALS * group
    ints = b_ints.reshape(8, ORBITALS, *b_ints.shape[1:])
    ints = lax.all_to_all(ints, OWN, 0, 0)

    ids = lax.dynamic_slice_in_dim(dom_blocks, first, ORBITALS, 0).reshape(16)
    fock = jnp.take(fock_tab, ids, axis=0, mode="clip").reshape(16, 64, 64)
    energy = jnp.take(vir_energy.reshape(-1, 64), ids, axis=0, mode="clip").reshape(16, 1, 64)
    occ = lax.dynamic_slice_in_dim(occ_energy, first, ORBITALS, 0)
    slots = ((pair_list - first) % 32).astype(jnp.int32)
    order = [block for half in HALVES for block in half]
    index_of = [order.index((i, j)) for i in range(ORBITALS) for j in range(ORBITALS)]
    index = jnp.take(
        jnp.array(index_of, jnp.int32), slots[:, 0] * ORBITALS + slots[:, 1], mode="clip"
    )
    w, den, rows = fock_terms(slots.reshape(-1), place, occ, fock, energy, t_amp)
    ints, index, w, den, rows = barrier((ints, index, w, den, rows))

    own, pieces = over_cores(*gram(place, ints, HALVES[0]))
    parts = over_x(pieces)
    own_b, pieces_b = over_cores(*gram(place, ints, HALVES[1]))
    parts_b = over_x(pieces_b)
    total = own + sum(to_float(part) for part in parts)
    near = swapped(total.astype(HALF), up)
    total = total + to_float(near)
    total_b = own_b + sum(to_float(part) for part in parts_b)
    total = total + to_float(swapped(total.astype(HALF), down))
    total_b = total_b + to_float(swapped(total_b.astype(HALF), down))
    total_b = total_b + to_float(swapped(total_b.astype(HALF), up))
    return finish(index, [total, total_b], w, den, rows)


def solution(mesh):
    fine = Mesh(mesh.devices.reshape(4, 2, 4, 2, 4), FIT + PAIR)
    placed = (
        P(None, FIT + PAIR, None),
        P(),
        P(PAIR, None),
        P(),
        P(),
        P(),
        P(PAIR, None, None),
    )
    return jax.shard_map(
        local,
        mesh=fine,
        in_specs=placed,
        out_specs=(P(PAIR, FIT, None), P(PAIR, FIT, None)),
        check_vma=False,
    )
```

time: 681 us -> 104 us (0.15)
  the two profiles are of different devices: /device:TPU:26 before, /device:TPU:32 now
where the time goes in v1:
time: 104 us; the launch traced here: 103 us
  waiting for transfers between devices  40.7 us (39%)
  starting transfers between devices  30.1 us (29%)
  Pallas kernels  18.7 us (18%)
  local copies, waits for them, and re-layouts  9.63 us (9%)
  other arithmetic  2.95 us (3%)
    all_to_all x1, waiting for transfers between devices, local(): ints = lax.all_to_all(ints, OWN, 0, 0)  26.7 us
    ppermute x4, starting transfers between devices, swapped(): return lax.ppermute(value, 'zq', [(i, partner(i) % 4) for i in range(4)])  13 us
    ppermute x4, waiting for transfers between devices, swapped(): return lax.ppermute(value, 'zq', [(i, partner(i) % 4) for i in range(4)])  11.8 us
    ppermute x8, starting transfers between devices, shifted(): lax.ppermute(value, axis, [(i, (i + by) % count) for i in range(count)])  10.7 us
    pallas_call x1, Pallas kernels, fock_terms(): pl.pallas_call(fock_kernel, out_shape=(out, out, out), grid_spec=pltpu.Pr...  8.56 us
    pallas_call x2, Pallas kernels, gram(): pl.pallas_call(functools.partial(gram_kernel, blocks), out_shape=[jax.Sha...  7.79 us
    all_to_all x1, starting transfers between devices, local(): ints = lax.all_to_all(ints, OWN, 0, 0)  6.42 us
    gather x1, local copies, waits for them, and re-layouts, local(): fock = jnp.take(fock_tab, ids, axis=0, mode='clip').reshape(16, 64, 64)  3.88 us
  transfers between devices with their start and end apart: 13, of which 7 were waited for; matrix products, arithmetic and copies ran while one was open for 11% of the time, Pallas kernels for 12%

profile of v1, /device:TPU:32, one launch (start us, length us, event | category | flops | bytes accessed | tf_op | source)
XLA Modules:
  0.0 102.8 jit_solution(14226612766310352491)
XLA Ops:
  0.6 0.0 copy-start
  0.6 0.0 copy-start.3
  0.7 0.0 copy-start.5
  0.7 0.0 copy-start.4
  0.7 0.0 copy-start.2
  0.7 6.4 %all-to-all-start = ((bf16[8,4,240,256]{3,2,1,0:T(8,128)(2,1)}), bf16[8,4,240,256]{3,2,1,0:T(8,128)(2,1)}, u32[]{:S(2)}, u32[]{:S(2)}) async-start(bf16[8,4,240,256]{3,2,1,0:T(8,128)(2,1)} %bitcast.48), calls=%async_computation | async-start | bytes 7864320 | tf_op jit(solution)/shard_map/all_to_all | solution.py:193
  7.1 0.0 copy-done
  7.1 0.1 constant_dynamic-slice_fusion
  7.2 0.1 copy.13
  7.3 0.1 reshape.60
  7.4 3.9 %gather_fusion.1 = bf16[16,4096]{1,0:T(8,128)(2,1)S(1)} fusion(bf16[625,4096]{1,0:T(8,128)(2,1)} %param.11, s32[1024]{0:T(1024)S(1)} %pad_clamp_fusion), kind=kCustom, calls=%fused_computation.1 | custom fusion | bytes 262208 | tf_op jit(solution)/shard_map/jit(_take)/gather | solution.py:196
  11.3 1.0 reshape.39.fock
  12.2 0.0 copy-done.3
  12.2 0.1 reshape.40
  12.4 1.2 %gather_fusion.2 = f32[16,64]{1,0:T(8,128)} fusion(f32[625,64]{1,0:T(8,128)S(1)} %reshape.40, s32[1024]{0:T(1024)S(1)} %pad_clamp_fusion), kind=kCustom, calls=%fused_computation.2 | custom fusion | bytes 8256 | tf_op jit(solution)/shard_map/jit(_take)/gather | solution.py:197
  13.5 0.0 copy-done.5
  13.5 0.6 dynamic_slice.6.occ
  14.1 0.0 copy-done.4
  14.1 0.1 copy.12
  14.2 0.7 reshape.38.slots
  14.9 0.0 copy-done.2
  14.9 1.2 %gather_fusion = s32[12]{0:T(128)} fusion(s32[16]{0:T(128)S(1)} %copy-done.2, s32[1024]{0:T(1024)S(1)} %pad_clamp_fusion.1), kind=kCustom, calls=%fused_computation | custom fusion | bytes 144 | tf_op jit(solution)/shard_map/jit(_take)/gather | solution.py:202
  16.1 0.6 pad_add_fusion.place
  16.8 8.6 %shard_map.95 = (f32[12,32,256]{2,1,0:T(8,128)}, f32[12,32,256]{2,1,0:T(8,128)}, f32[12,32,256]{2,1,0:T(8,128)}) custom-call(s32[24]{0:T(128)} %reshape.38.slots, s32[4]{0:T(128)} %pad_add_fusion.place, f32[4]{0:T(128)} %dynamic_slice.6.occ, bf16[16,64,64]{2,1,0:T(8,128)(2,1)} %reshape.39.fock, f32[16,1,64]{2,1,0:T(1,128)} %bitcast.49, bf16[12,256,256]{2,1,0:T(8,128)(2,1)} %amp.1), custom_call_target="tpu_custom_call" | custom-call | flops 25165824 | bytes 1572864 | tf_op jit(solution)/shard_map/pallas_call | solution.py:123
  25.3 26.7 %all-to-all-done.ints = bf16[8,4,240,256]{3,2,1,0:T(8,128)(2,1)} async-done(((bf16[8,4,240,256]{3,2,1,0:T(8,128)(2,1)}), bf16[8,4,240,256]{3,2,1,0:T(8,128)(2,1)}, u32[]{:S(2)}, u32[]{:S(2)}) %all-to-all-start) | async-done | bytes 3932192 | tf_op jit(solution)/shard_map/all_to_all | solution.py:193
  52.0 0.0 copy-start.1
  52.0 0.7 copy-done.1
  52.7 3.9 %shard_map.97 = (f32[8,32,256]{2,1,0:T(8,128)S(1)}, f32[8,32,256]{2,1,0:T(8,128)S(1)}, f32[8,32,256]{2,1,0:T(8,128)S(1)}, f32[8,32,256]{2,1,0:T(8,128)S(1)}, f32[4,8,32,256]{3,2,1,0:T(8,128)S(1)}) custom-call(s32[4]{0:T(128)S(1)} %copy-done.1, bf16[8,4,240,256]{3,2,1,0:T(8,128)(2,1)} %all-to-all-done.ints), custom_call_target="tpu_custom_call" | custom-call | flops 2013265920 | bytes 4194304 | tf_op jit(solution)/shard_map/pallas_call | solution.py:67
  56.6 0.1 convert_element_type.133
  56.7 0.1 collective-permute-start.6
  56.8 3.9 %shard_map.96 = (f32[8,32,256]{2,1,0:T(8,128)S(1)}, f32[8,32,256]{2,1,0:T(8,128)S(1)}, f32[8,32,256]{2,1,0:T(8,128)S(1)}, f32[8,32,256]{2,1,0:T(8,128)S(1)}, f32[4,8,32,256]{3,2,1,0:T(8,128)S(1)}) custom-call(s32[4]{0:T(128)S(1)} %copy-done.1, bf16[8,4,240,256]{3,2,1,0:T(8,128)(2,1)} %all-to-all-done.ints), custom_call_target="tpu_custom_call" | custom-call | flops 2013265920 | bytes 4194304 | tf_op jit(solution)/shard_map/pallas_call | solution.py:67
  60.7 0.1 convert_element_type.114
  60.8 0.6 collective-permute-start
  61.4 0.0 collective-permute-done.6
  61.4 0.1 fusion.2
  61.5 3.1 %collective-permute-start.7 = (f16[8,32,256]{2,1,0:T(8,128)(2,1)S(1)}, f16[8,32,256]{2,1,0:T(8,128)(2,1)S(1)}, u32[]{:S(2)}, u32[]{:S(2)}) collective-permute-start(f16[8,32,256]{2,1,0:T(8,128)(2,1)S(1)} %get-tuple-element.42), channel_id=1, source_target_pairs={{0,128},{64,192},{128,0},{192,64},{1,129},{65,193},{129,1},{193,65... | collective-permute-start | bytes 393224 | tf_op jit(solution)/shard_map/ppermute | solution.py:170
  64.6 0.6 collective-permute-start.8
  65.3 2.6 %collective-permute-start.9 = (f16[8,32,256]{2,1,0:T(8,128)(2,1)S(1)}, f16[8,32,256]{2,1,0:T(8,128)(2,1)S(1)}, u32[]{:S(2)}, u32[]{:S(2)}) collective-permute-start(f16[8,32,256]{2,1,0:T(8,128)(2,1)S(1)} %get-tuple-element.43), channel_id=1, source_target_pairs={{0,192},{64,0},{128,64},{192,128},{1,193},{65,1},{129,65},{193,129... | collective-permute-start | bytes 393224 | tf_op jit(solution)/shard_map/ppermute | solution.py:170
  67.9 0.0 collective-permute-done
  67.9 0.1 fusion.6
  68.0 0.1 collective-permute-start.1
  68.1 0.8 collective-permute-start.2
  69.0 0.5 collective-permute-done.7
  69.5 2.8 %collective-permute-start.3 = (f16[8,32,256]{2,1,0:T(8,128)(2,1)S(1)}, f16[8,32,256]{2,1,0:T(8,128)(2,1)S(1)}, u32[]{:S(2)}, u32[]{:S(2)}) collective-permute-start(f16[8,32,256]{2,1,0:T(8,128)(2,1)S(1)} %get-tuple-element.46), channel_id=1, source_target_pairs={{0,192},{64,0},{128,64},{192,128},{1,193},{65,1},{129,65},{193,129... | collective-permute-start | bytes 393224 | tf_op jit(solution)/shard_map/ppermute | solution.py:170
  72.3 1.4 %collective-permute-done.8 = f16[8,32,256]{2,1,0:T(8,128)(2,1)S(1)} collective-permute-done((f16[8,32,256]{2,1,0:T(8,128)(2,1)S(1)}, f16[8,32,256]{2,1,0:T(8,128)(2,1)S(1)}, u32[]{:S(2)}, u32[]{:S(2)}) %collective-permute-start.8) | collective-permute-done | bytes 131104 | tf_op jit(solution)/shard_map/ppermute | solution.py:170
  73.7 0.3 collective-permute-done.9
  73.9 0.1 fusion.11
  74.0 5.5 %collective-permute-start.10 = (f16[8,32,256]{2,1,0:T(8,128)(2,1)S(1)}, f16[8,32,256]{2,1,0:T(8,128)(2,1)S(1)}, u32[]{:S(2)}, u32[]{:S(2)}) collective-permute-start(f16[8,32,256]{2,1,0:T(8,128)(2,1)S(1)} %get-tuple-element.38), channel_id=1, source_target_pairs={{0,24},{8,16},{16,8},{24,0},{1,25},{9,17},{17,9},{25,1},{2,26},{10... | collective-permute-start | bytes 393224 | tf_op jit(solution)/shard_map/ppermute | solution.py:33
  79.6 0.0 collective-permute-done.1
  79.6 0.0 collective-permute-done.2
  79.6 0.0 collective-permute-done.3
  79.6 0.1 fusion.13
  79.7 1.5 %collective-permute-start.4 = (f16[8,32,256]{2,1,0:T(8,128)(2,1)S(1)}, f16[8,32,256]{2,1,0:T(8,128)(2,1)S(1)}, u32[]{:S(2)}, u32[]{:S(2)}) collective-permute-start(f16[8,32,256]{2,1,0:T(8,128)(2,1)S(1)} %get-tuple-element.40), channel_id=1, source_target_pairs={{0,8},{8,0},{16,24},{24,16},{1,9},{9,1},{17,25},{25,17},{2,10},{10... | collective-permute-start | bytes 393224 | tf_op jit(solution)/shard_map/ppermute | solution.py:33
  81.2 2.8 %collective-permute-done.10 = f16[8,32,256]{2,1,0:T(8,128)(2,1)S(1)} collective-permute-done((f16[8,32,256]{2,1,0:T(8,128)(2,1)S(1)}, f16[8,32,256]{2,1,0:T(8,128)(2,1)S(1)}, u32[]{:S(2)}, u32[]{:S(2)}) %collective-permute-start.10) | collective-permute-done | bytes 131104 | tf_op jit(solution)/shard_map/ppermute | solution.py:33
  84.0 1.0 collective-permute-start.11
  85.0 4.7 %collective-permute-done.4 = f16[8,32,256]{2,1,0:T(8,128)(2,1)S(1)} collective-permute-done((f16[8,32,256]{2,1,0:T(8,128)(2,1)S(1)}, f16[8,32,256]{2,1,0:T(8,128)(2,1)S(1)}, u32[]{:S(2)}, u32[]{:S(2)}) %collective-permute-start.4) | collective-permute-done | bytes 131104 | tf_op jit(solution)/shard_map/ppermute | solution.py:33
  89.8 5.0 %collective-permute-start.5 = (f16[8,32,256]{2,1,0:T(8,128)(2,1)S(1)}, f16[8,32,256]{2,1,0:T(8,128)(2,1)S(1)}, u32[]{:S(2)}, u32[]{:S(2)}) collective-permute-start(f16[8,32,256]{2,1,0:T(8,128)(2,1)S(1)} %fusion.8), channel_id=1, source_target_pairs={{0,24},{8,16},{16,8},{24,0},{1,25},{9,17},{17,9},{25,1},{2,26},{10... | collective-permute-start | bytes 393224 | tf_op jit(solution)/shard_map/ppermute | solution.py:33
  94.7 0.0 collective-permute-done.11
  94.7 0.7 convert_add_fusion.8.b_ref
  95.5 4.2 %collective-permute-done.5 = f16[8,32,256]{2,1,0:T(8,128)(2,1)S(1)} collective-permute-done((f16[8,32,256]{2,1,0:T(8,128)(2,1)S(1)}, f16[8,32,256]{2,1,0:T(8,128)(2,1)S(1)}, u32[]{:S(2)}, u32[]{:S(2)}) %collective-permute-start.5) | collective-permute-done | bytes 131104 | tf_op jit(solution)/shard_map/ppermute | solution.py:33
  99.7 0.7 convert_add_fusion.10.a_ref
  100.5 2.3 %shard_map.98 = (f32[12,32,256]{2,1,0:T(8,128)}, bf16[12,32,256]{2,1,0:T(8,128)(2,1)}) custom-call(s32[12]{0:T(128)} %gather_fusion, f32[8,32,256]{2,1,0:T(8,128)} %convert_add_fusion.10.a_ref, f32[8,32,256]{2,1,0:T(8,128)} %convert_add_fusion.8.b_ref, f32[12,32,256]{2,1,0:T(8,128)} %get-tuple-element.35.w_ref, f32[12,32,256]{2,1,0:T(8,128)} %get-tuple-element.36.den_ref, ...), custom_call_target="tpu_custom_call" | custom-call | tf_op jit(solution)/shard_map/pallas_call | solution.py:156
  (6 shorter events, 0.1 us)
Async XLA Ops:
  0.6 6.5 %copy-start = (s32[32,4]{0,1:T(4,128)S(1)}, s32[32,4]{0,1:T(4,128)}, u32[]{:S(2)}) copy-start(s32[32,4]{0,1:T(4,128)} %param.9) | copy-start | bytes 1540
  0.6 11.6 %copy-start.3 = (f32[40000]{0:T(1024)S(1)}, f32[40000]{0:T(1024)}, u32[]{:S(2)}) copy-start(f32[40000]{0:T(1024)} %param.12) | copy-start | bytes 480004
  0.7 12.9 %copy-start.5 = (f32[32]{0:T(128)S(1)}, f32[32]{0:T(128)}, u32[]{:S(2)}) copy-start(f32[32]{0:T(128)} %param.13) | copy-start | bytes 388
  0.7 13.4 %copy-start.4 = (s32[12,2]{0,1:T(2,128)S(1)}, s32[12,2]{0,1:T(2,128)}, u32[]{:S(2)}) copy-start(s32[12,2]{0,1:T(2,128)} %param.10) | copy-start | bytes 292
  0.7 14.2 %copy-start.2 = (s32[16]{0:T(128)S(1)}, s32[16]{0:T(128)}, u32[]{:S(2)}) copy-start(s32[16]{0:T(128)} %constant.38.clone) | copy-start | bytes 196
  0.7 51.3 %all-to-all-start = ((bf16[8,4,240,256]{3,2,1,0:T(8,128)(2,1)}), bf16[8,4,240,256]{3,2,1,0:T(8,128)(2,1)}, u32[]{:S(2)}, u32[]{:S(2)}) async-start(bf16[8,4,240,256]{3,2,1,0:T(8,128)(2,1)} %bitcast.48), calls=%async_computation | async-start | bytes 7864320 | tf_op jit(solution)/shard_map/all_to_all | solution.py:193
  52.0 0.7 copy-start.1
  56.7 4.7 %collective-permute-start.6 = (f16[4,8,32,256]{3,2,1,0:T(8,128)(2,1)S(1)}, f16[4,8,32,256]{3,2,1,0:T(8,128)(2,1)S(1)}, u32[]{:S(2)}, u32[]{:S(2)}) collective-permute-start(f16[4,8,32,256]{3,2,1,0:T(8,128)(2,1)S(1)} %convert_element_type.133), channel_id=1, source_target_pairs={{0,32},{32,0},{1,33},{33,1},{2,34},{34,2},{3,35},{35,3},{4,36},{36... | collective-permute-start | bytes 1572872 | tf_op jit(solution)/shard_map/ppermute | solution.py:170
  60.8 7.1 %collective-permute-start = (f16[4,8,32,256]{3,2,1,0:T(8,128)(2,1)S(1)}, f16[4,8,32,256]{3,2,1,0:T(8,128)(2,1)S(1)}, u32[]{:S(2)}, u32[]{:S(2)}) collective-permute-start(f16[4,8,32,256]{3,2,1,0:T(8,128)(2,1)S(1)} %convert_element_type.114), channel_id=1, source_target_pairs={{0,32},{32,0},{1,33},{33,1},{2,34},{34,2},{3,35},{35,3},{4,36},{36... | collective-permute-start | bytes 1572872 | tf_op jit(solution)/shard_map/ppermute | solution.py:170
  61.5 8.0 %collective-permute-start.7 = (f16[8,32,256]{2,1,0:T(8,128)(2,1)S(1)}, f16[8,32,256]{2,1,0:T(8,128)(2,1)S(1)}, u32[]{:S(2)}, u32[]{:S(2)}) collective-permute-start(f16[8,32,256]{2,1,0:T(8,128)(2,1)S(1)} %get-tuple-element.42), channel_id=1, source_target_pairs={{0,128},{64,192},{128,0},{192,64},{1,129},{65,193},{129,1},{193,65... | collective-permute-start | bytes 393224 | tf_op jit(solution)/shard_map/ppermute | solution.py:170
  64.6 9.0 %collective-permute-start.8 = (f16[8,32,256]{2,1,0:T(8,128)(2,1)S(1)}, f16[8,32,256]{2,1,0:T(8,128)(2,1)S(1)}, u32[]{:S(2)}, u32[]{:S(2)}) collective-permute-start(f16[8,32,256]{2,1,0:T(8,128)(2,1)S(1)} %get-tuple-element.44), channel_id=1, source_target_pairs={{0,64},{64,128},{128,192},{192,0},{1,65},{65,129},{129,193},{193,1... | collective-permute-start | bytes 393224 | tf_op jit(solution)/shard_map/ppermute | solution.py:170
  65.3 8.7 %collective-permute-start.9 = (f16[8,32,256]{2,1,0:T(8,128)(2,1)S(1)}, f16[8,32,256]{2,1,0:T(8,128)(2,1)S(1)}, u32[]{:S(2)}, u32[]{:S(2)}) collective-permute-start(f16[8,32,256]{2,1,0:T(8,128)(2,1)S(1)} %get-tuple-element.43), channel_id=1, source_target_pairs={{0,192},{64,0},{128,64},{192,128},{1,193},{65,1},{129,65},{193,129... | collective-permute-start | bytes 393224 | tf_op jit(solution)/shard_map/ppermute | solution.py:170
  68.0 11.5 %collective-permute-start.1 = (f16[8,32,256]{2,1,0:T(8,128)(2,1)S(1)}, f16[8,32,256]{2,1,0:T(8,128)(2,1)S(1)}, u32[]{:S(2)}, u32[]{:S(2)}) collective-permute-start(f16[8,32,256]{2,1,0:T(8,128)(2,1)S(1)} %get-tuple-element.45), channel_id=1, source_target_pairs={{0,128},{64,192},{128,0},{192,64},{1,129},{65,193},{129,1},{193,65... | collective-permute-start | bytes 393224 | tf_op jit(solution)/shard_map/ppermute | solution.py:170
  68.1 11.4 %collective-permute-start.2 = (f16[8,32,256]{2,1,0:T(8,128)(2,1)S(1)}, f16[8,32,256]{2,1,0:T(8,128)(2,1)S(1)}, u32[]{:S(2)}, u32[]{:S(2)}) collective-permute-start(f16[8,32,256]{2,1,0:T(8,128)(2,1)S(1)} %get-tuple-element.47), channel_id=1, source_target_pairs={{0,64},{64,128},{128,192},{192,0},{1,65},{65,129},{129,193},{193,1... | collective-permute-start | bytes 393224 | tf_op jit(solution)/shard_map/ppermute | solution.py:170
  69.5 10.1 %collective-permute-start.3 = (f16[8,32,256]{2,1,0:T(8,128)(2,1)S(1)}, f16[8,32,256]{2,1,0:T(8,128)(2,1)S(1)}, u32[]{:S(2)}, u32[]{:S(2)}) collective-permute-start(f16[8,32,256]{2,1,0:T(8,128)(2,1)S(1)} %get-tuple-element.46), channel_id=1, source_target_pairs={{0,192},{64,0},{128,64},{192,128},{1,193},{65,1},{129,65},{193,129... | collective-permute-start | bytes 393224 | tf_op jit(solution)/shard_map/ppermute | solution.py:170
  74.0 9.9 %collective-permute-start.10 = (f16[8,32,256]{2,1,0:T(8,128)(2,1)S(1)}, f16[8,32,256]{2,1,0:T(8,128)(2,1)S(1)}, u32[]{:S(2)}, u32[]{:S(2)}) collective-permute-start(f16[8,32,256]{2,1,0:T(8,128)(2,1)S(1)} %get-tuple-element.38), channel_id=1, source_target_pairs={{0,24},{8,16},{16,8},{24,0},{1,25},{9,17},{17,9},{25,1},{2,26},{10... | collective-permute-start | bytes 393224 | tf_op jit(solution)/shard_map/ppermute | solution.py:33
  79.7 10.1 %collective-permute-start.4 = (f16[8,32,256]{2,1,0:T(8,128)(2,1)S(1)}, f16[8,32,256]{2,1,0:T(8,128)(2,1)S(1)}, u32[]{:S(2)}, u32[]{:S(2)}) collective-permute-start(f16[8,32,256]{2,1,0:T(8,128)(2,1)S(1)} %get-tuple-element.40), channel_id=1, source_target_pairs={{0,8},{8,0},{16,24},{24,16},{1,9},{9,1},{17,25},{25,17},{2,10},{10... | collective-permute-start | bytes 393224 | tf_op jit(solution)/shard_map/ppermute | solution.py:33
  84.0 10.7 %collective-permute-start.11 = (f16[8,32,256]{2,1,0:T(8,128)(2,1)S(1)}, f16[8,32,256]{2,1,0:T(8,128)(2,1)S(1)}, u32[]{:S(2)}, u32[]{:S(2)}) collective-permute-start(f16[8,32,256]{2,1,0:T(8,128)(2,1)S(1)} %fusion.9), channel_id=1, source_target_pairs={{0,8},{8,0},{16,24},{24,16},{1,9},{9,1},{17,25},{25,17},{2,10},{10... | collective-permute-start | bytes 393224 | tf_op jit(solution)/shard_map/ppermute | solution.py:33
  89.8 9.9 %collective-permute-start.5 = (f16[8,32,256]{2,1,0:T(8,128)(2,1)S(1)}, f16[8,32,256]{2,1,0:T(8,128)(2,1)S(1)}, u32[]{:S(2)}, u32[]{:S(2)}) collective-permute-start(f16[8,32,256]{2,1,0:T(8,128)(2,1)S(1)} %fusion.8), channel_id=1, source_target_pairs={{0,24},{8,16},{16,8},{24,0},{1,25},{9,17},{17,9},{25,1},{2,26},{10... | collective-permute-start | bytes 393224 | tf_op jit(solution)/shard_map/ppermute | solution.py:33
